TPU v7x, 32 devices: a whole 2x2x4 slice. The times are simulated.
32 devices in a mesh: ka: 4 (over x, core), ga: 8 (over z, y).
Axes of the slice: x: 2, y: 2, z: 4, core: 2. Of those that a mesh axis runs over, the one named last changes fastest.
Arguments:
- pair_vc: bfloat16 [384, 2048, 128], P('ka', 'ga'), may hold values from -6 to 6
- coulomb: float32 [2048], P('ga'), may hold values from 0.01 to 0.1
- dens_cc: bfloat16 [2, 384, 2048, 128], P(None, 'ka', 'ga'), may hold values from -1.5 to 1.5
- dens_vv: bfloat16 [2, 384, 2048, 128], P(None, 'ka', 'ga'), may hold values from -1.5 to 1.5
- screen: bfloat16 [2, 2048, 2048], P(None, 'ga'), may hold values from -0.125 to 0.125
- offsets: int32 [2, 2], replicated, may hold values from 0 to 23, as said below
Outputs:
- kernel: float32 [2, 2, 384, 4096], P(None, None, ('ka', 'ga'))
Inputs may be any that keep to these rules, and one draw needn't show every extreme that they name: offsets[o, 0] is 1 to 4; one offset, which one drawn from the seed, has offsets[o, 0] = 4 and offsets[o, 1] = 23, the other has offsets[o, 1] = 0.
All inputs are finite; a program needn't handle non-finite values.
Results may differ from a plain program's by a relative error of at most 0.0029.
Values may be sent and summed in bfloat16 or wider, within the bound.
A program may use at most 192 MiB of HBM per device.

v0:
```python
import jax
import jax.numpy as jnp
from jax import lax
from jax.sharding import PartitionSpec as P

NV = 8
NC = 8
NKY = 24
KX_DEV = 4
NOFF = 2


def from_behind(array, axis, by):
    length = lax.axis_size(axis)
    return lax.ppermute(array, axis, [(i, (i + by) % length) for i in range(length)])


def shifted_rows(joined, step_x, step_y):
    picked = lax.dynamic_slice_in_dim(joined, step_x, KX_DEV, 0)
    twice = jnp.concatenate([picked, picked], axis=1)
    return lax.dynamic_slice_in_dim(twice, step_y, NKY, 1)


def pair_products(left_side, right_side):
    left_half = left_side.shape[-1] // 2
    right_half = right_side.shape[-1] // 2
    full = jnp.einsum("kgp,kgq->kpq", left_side, right_side, preferred_element_type=jnp.float32)
    real_part = full[:, :left_half, :right_half] + full[:, left_half:, right_half:]
    imag_part = full[:, :left_half, right_half:] - full[:, left_half:, :right_half]
    return jnp.stack([real_part, imag_part])


def summed_exchange(scaled, moved):
    partial_terms = jnp.stack(
        [pair_products(scaled, moved[offset_index]) for offset_index in range(NOFF)]
    )
    return lax.psum_scatter(partial_terms, "ga", scatter_dimension=2, tiled=True)


def local(pair_vc, coulomb, dens_cc, dens_vv, screen, offsets):
    local_k = pair_vc.shape[0]
    slab = pair_vc.shape[1]
    width = pair_vc.shape[2]
    pairs = width // 2
    shards = lax.axis_size("ga")
    few_k = local_k // shards
    scaled = (coulomb[None, :, None] * pair_vc.astype(jnp.float32)).astype(jnp.bfloat16)
    ahead = from_behind(pair_vc, "ka", -1)
    joined = jnp.concatenate([pair_vc, ahead], axis=0).reshape(2 * KX_DEV, NKY, slab, width)
    moved = jnp.stack(
        [
            shifted_rows(joined, offsets[offset_index, 0], offsets[offset_index, 1]).reshape(
                local_k, slab, width
            )
            for offset_index in range(NOFF)
        ]
    )
    cc_x, vv_x = (
        lax.all_to_all(dens_cc, "ga", split_axis=1, concat_axis=2, tiled=True),
        lax.all_to_all(dens_vv, "ga", split_axis=1, concat_axis=2, tiled=True),
    )
    exch = summed_exchange(scaled, moved)
    blocks = []
    for offset_index in range(NOFF):
        mc_here = cc_x[offset_index]
        mv_here = vv_x[offset_index]

        def add_one(carry, piece, start, mc_here=mc_here, mv_here=mv_here):
            image = jnp.einsum(
                "gh,khq->kgq", piece, mv_here, preferred_element_type=jnp.float32
            ).astype(jnp.bfloat16)
            return pair_products(mc_here, image)

        zeros_one = jnp.zeros((2, few_k, NC * NC, NV * NV), jnp.float32)
        blocks.append(
            add_one(
                zeros_one,
                lax.all_gather(screen[offset_index], "ga", axis=0, tiled=True),
                jnp.int32(0),
            )
        )
    direct = jnp.stack(blocks)
    shaped = direct.reshape(NOFF, 2, few_k, NC, NC, NV, NV)
    shaped = jnp.transpose(shaped, (0, 1, 2, 5, 3, 6, 4)).reshape(NOFF, 2, few_k, pairs * pairs)
    return 2.0 * exch.reshape(NOFF, 2, few_k, pairs * pairs) - shaped


def solution(mesh):
    placed = (
        P("ka", "ga", None),
        P("ga"),
        P(None, "ka", "ga", None),
        P(None, "ka", "ga", None),
        P(None, "ga", None),
        P(),
    )
    return jax.shard_map(
        local,
        mesh=mesh,
        in_specs=placed,
        out_specs=P(None, None, ("ka", "ga"), None),
        check_vma=False,
    )
```

profile of v0, /device:TPU:13, one launch (start us, length us, event | category | flops | bytes accessed | tf_op | source)
XLA Modules:
  0.0 1235.2 jit_solution(13315231768000676614)
XLA Ops:
  6.5 10.7 copy.41
  17.2 5.8 all-to-all-start.1
  32.1 62.6 %collective-permute-done = bf16[96,256,128]{2,1,0:T(8,128)(2,1)} collective-permute-done((bf16[96,256,128]{2,1,0:T(8,128)(2,1)}, bf16[96,256,128]{2,1,0:T(8,128)(2,1)}, u32[]{:S(2)}, u32[]{:S(2)}) %collective-permute-start) | collective-permute-done | bytes 6291488 | tf_op jit(solution)/shard_map/ppermute | solution.py:15
  94.6 12.2 pad_maximum_fusion
  106.8 14.5 %constant_dynamic-slice_fusion.1 = (bf16[4,24,256,128]{3,2,1,0:T(8,128)(2,1)}, bf16[4,24,256,128]{3,2,1,0:T(8,128)(2,1)}) fusion(bf16[8,24,256,128]{3,2,1,0:T(8,128)(2,1)} %bitcast.70, s32[]{:T(128)S(6)} %select_n.12, s32[]{:T(128)S(6)} %select_n.14), kind=kLoop, calls=%fused_computation.40 | loop fusion | bytes 25165832 | tf_op jit(solution)/shard_map/dynamic_slice | solution.py:19
  121.3 12.8 %fusion.4 = (bf16[4,24,256,128]{3,2,1,0:T(8,128)(2,1)}, bf16[4,24,256,128]{3,2,1,0:T(8,128)(2,1)}) fusion(s32[]{:T(128)S(6)} %select_n.15, bf16[4,24,256,128]{3,2,1,0:T(8,128)(2,1)} %get-tuple-element.6, s32[]{:T(128)S(6)} %select_n.13, bf16[4,24,256,128]{3,2,1,0:T(8,128)(2,1)} %get-tuple-element.5), kind=kLoop, calls=%fused_computation.13 | loop fusion | flops 6291456 | bytes 25165832 | tf_op jit(solution)/shard_map/concatenate | solution.py:20
  134.2 5.1 fusion.14
  142.6 5.6 maximum_bitcast_fusion.2
  156.6 5.7 maximum_bitcast_fusion.1
  162.3 9.6 pad_maximum_fusion.1
  175.0 10.8 copy.37
  185.8 243.5 %all-to-all-done.1 = bf16[2,96,256,128]{3,2,0,1:T(8,128)(2,1)} async-done(((bf16[2,96,256,128]{3,2,0,1:T(8,128)(2,1)}), bf16[2,96,256,128]{3,2,0,1:T(8,128)(2,1)}, u32[]{:S(2)}, u32[]{:S(2)}) %all-to-all-start.1) | async-done | bytes 12582944 | tf_op jit(solution)/shard_map/all_to_all | solution.py:59
  429.3 6.9 all-to-all-start
  438.2 473.1 %all-reduce.3.cloned.1.call-done = f32[2,2,96,64,64]{4,3,2,1,0:T(8,128)} async-done(((f32[2,2,96,64,64]{4,3,2,1,0:T(8,128)}), f32[2,2,96,64,64]{4,3,2,1,0:T(8,128)}) %all-reduce.3.cloned.1.call-update) | async-done | bytes 6291472
  914.4 10.8 copy.59
  925.2 6.6 copy.38
  946.0 91.0 %all-gather.7.cloned.1.call-done = bf16[1,2048,2048]{2,1,0:T(8,128)(2,1)} async-done(((bf16[1,256,2048]{2,1,0:T(8,128)(2,1)}), bf16[1,2048,2048]{2,1,0:T(8,128)(2,1)}) %all-gather.7.cloned.1.call-update) | async-done | bytes 8388624 | tf_op jit(solution)/shard_map/all_gather | solution.py:78
  1037.0 20.3 %fusion.19 = f32[12,128,128]{1,2,0:T(8,128)S(1)} fusion(bf16[12,2048,128]{2,1,0:T(8,128)(2,1)} %bitcast.77, bf16[12,2048,128]{2,1,0:T(8,128)(2,1)} %bitcast.74, bf16[1,2048,2048]{2,1,0:T(8,128)(2,1)} %all-gather.7.cloned.1.call-done), kind=kOutput, calls=%fused_computation.33 | convolution fusion | flops 13690208256 | bytes 21757952 | tf_op jit(solution)/shard_map/kgp,kgq->kpq/dot_general | solution.py:27
  1064.7 6.2 copy.39
  1070.9 91.6 %all-gather.5.cloned.1.call-done = bf16[1,2048,2048]{2,1,0:T(8,128)(2,1)} async-done(((bf16[1,256,2048]{2,1,0:T(8,128)(2,1)}), bf16[1,2048,2048]{2,1,0:T(8,128)(2,1)}) %all-gather.5.cloned.1.call-update) | async-done | bytes 8388624 | tf_op jit(solution)/shard_map/all_gather | solution.py:78
  1162.5 21.0 %fusion.16 = f32[12,128,128]{1,2,0:T(8,128)} fusion(bf16[12,2048,128]{2,1,0:T(8,128)(2,1)} %bitcast.76, bf16[12,2048,128]{2,1,0:T(8,128)(2,1)} %bitcast.75, bf16[1,2048,2048]{2,1,0:T(8,128)(2,1)} %all-gather.5.cloned.1.call-done), kind=kOutput, calls=%fused_computation.32 | convolution fusion | flops 13690208256 | bytes 21757952 | tf_op jit(solution)/shard_map/kgp,kgq->kpq/dot_general | solution.py:27
  1195.1 9.6 maximum_bitcast_fusion
  1204.7 12.7 %copy.49 = f32[2,2,12,8,8,8,8]{6,5,4,3,1,2,0:T(8,128)} copy(f32[2,2,12,8,8,8,8]{5,3,6,4,2,1,0:T(8,128)} %maximum_bitcast_fusion) | data formatting | bytes 1572864 | tf_op jit(solution)/shard_map/transpose | solution.py:84
  1217.4 9.4 reshape.32
  (54 shorter events, 55.8 us)
Async XLA Ops:
  17.2 7.0 copy-start.4
  17.2 412.1 %all-to-all-start.1 = ((bf16[2,96,256,128]{3,2,0,1:T(8,128)(2,1)}), bf16[2,96,256,128]{3,2,0,1:T(8,128)(2,1)}, u32[]{:S(2)}, u32[]{:S(2)}) async-start(bf16[2,96,256,128]{3,2,0,1:T(8,128)(2,1)} %copy.41), calls=%async_computation.1 | async-start | bytes 25165824 | tf_op jit(solution)/shard_map/all_to_all | solution.py:59
  23.0 888.3 %all-reduce.3.cloned.1.call-start = ((), (), s32[]{:S(2)}) async-start(), calls=%async_computation.4 | async-start | bytes 25165824
  23.0 71.6 %collective-permute-start = (bf16[96,256,128]{2,1,0:T(8,128)(2,1)}, bf16[96,256,128]{2,1,0:T(8,128)(2,1)}, u32[]{:S(2)}, u32[]{:S(2)}) collective-permute-start(bf16[96,256,128]{2,1,0:T(8,128)(2,1)} %param.6), channel_id=1, source_target_pairs={{0,24},{8,0},{16,8},{24,16},{1,25},{9,1},{17,9},{25,17},{2,26},{10... | collective-permute-start | bytes 18874376 | tf_op jit(solution)/shard_map/ppermute | solution.py:15
  106.8 27.3 %slice-start = ((s8[6291456]{0:T(1024)(128)(4,1)}), s8[2097152]{0:T(1024)(128)(4,1)S(1)}, s32[]{:S(2)}) async-start(s8[6291456]{0:T(1024)(128)(4,1)} %bitcast.65), calls=%async_computation.5 | async-start | bytes 4194304
  121.3 12.8 %slice-start.1 = ((s8[6291456]{0:T(1024)(128)(4,1)}), s8[4194304]{0:T(1024)(128)(4,1)S(1)}, s32[]{:S(2)}) async-start(s8[6291456]{0:T(1024)(128)(4,1)} %bitcast.65), calls=%async_computation.6 | async-start | bytes 8388608
  121.3 12.8 %copy-start.3 = (f32[256]{0:T(256)S(1)}, f32[256]{0:T(256)}, u32[]{:S(2)}) copy-start(f32[256]{0:T(256)} %param.7) | copy-start | bytes 3076
  156.6 5.7 copy-start
  171.9 1.6 copy-start.2
  171.9 865.1 %all-gather.7.cloned.1.call-start = ((), (), s32[]{:S(2)}) async-start(), calls=%async_computation.3 | async-start | bytes 9437184 | tf_op jit(solution)/shard_map/all_gather | solution.py:78
  185.8 251.2 %copy-start.5 = (u32[32]{0:T(128)S(1)}, u32[32]{0:T(128)}, u32[]{:S(2)}) copy-start(u32[32]{0:T(128)} %constant.10) | copy-start | bytes 388
  429.3 495.9 %all-to-all-start = ((bf16[2,96,256,128]{3,2,0,1:T(8,128)(2,1)}), bf16[2,96,256,128]{3,2,0,1:T(8,128)(2,1)}, u32[]{:S(2)}, u32[]{:S(2)}) async-start(bf16[2,96,256,128]{3,2,0,1:T(8,128)(2,1)} %copy.37), calls=%async_computation | async-start | bytes 25165824 | tf_op jit(solution)/shard_map/all_to_all | solution.py:60
  436.2 726.3 %all-gather.5.cloned.1.call-start = ((), (), s32[]{:S(2)}) async-start(), calls=%async_computation.2 | async-start | bytes 9437184 | tf_op jit(solution)/shard_map/all_gather | solution.py:78
  931.8 7.8 slice-start.2
  931.8 7.8 slice-start.3
  935.9 5.2 slice-start.4
  1217.4 9.4 copy-start.1
Sparse Core Ops, SparseCore 0:
  172.0 739.2 all-reduce.2
  913.7 123.2 all-gather.6
  1039.3 123.1 all-gather.4
where the time goes:
time: 1250 us; the launch traced here: 1240 us
  waiting for transfers between devices  963 us (77%)
  local copies, waits for them, and re-layouts  118 us (9%)
  other arithmetic  68 us (5%)
  matrix products  51.5 us (4%)
  between operations  21.3 us (2%)
  starting transfers between devices  14 us (1%)
    unnamed x4, waiting for transfers between devices  474 us
    all_to_all x1, waiting for transfers between devices, local(): lax.all_to_all(dens_cc, 'ga', split_axis=1, concat_axis=2, tiled=True)  244 us
    all_gather x2, waiting for transfers between devices, local(): lax.all_gather(screen[offset_index], 'ga', axis=0, tiled=True)  183 us
    ppermute x1, waiting for transfers between devices, from_behind(): lax.ppermute(array, axis, [(i, (i + by) % length) for i in range(length)])  62.6 us
    dot_general x4, matrix products, pair_products(): jnp.einsum('kgp,kgq->kpq', left_side, right_side, preferred_element_type=...  51.5 us
    unnamed x25, local copies, waits for them, and re-layouts  25.2 us
  transfers between devices with their start and end apart: 6, of which 5 were waited for; matrix products, arithmetic and copies ran while one was open for 13% of the time, Pallas kernels for 0%

commit v1 on v0

v1 whole, which is shorter than its diff:
```python
import functools

import jax
import jax.numpy as jnp
from jax import lax
from jax.experimental import pallas as pl
from jax.experimental.pallas import tpu as pltpu
from jax.sharding import PartitionSpec as P

NV = 8
NC = 8
NKY = 24
NOFF = 2
WINDOW = 10
MESH = pl.DeviceIdType.MESH


def step_order(length):
    order = []
    for i in range(length):
        step = length // 2 + (i + 1) // 2 * (1 if i % 2 else -1)
        if 0 < step < length:
            order.append(step)
    return order


def over_rows(left, right):
    return lax.dot_general(
        left, right, (((0,), (0,)), ((), ())), preferred_element_type=jnp.float32
    )


def block_transpose(tile):
    row = lax.broadcasted_iota(jnp.int32, tile.shape, 1)
    lane = lax.broadcasted_iota(jnp.int32, tile.shape, 2)
    for bit in range(3):
        size = 1 << bit
        row_bit = (row // size) % 2
        lane_bit = (lane // (8 * size)) % 2
        down = pltpu.roll(pltpu.roll(tile, 8 - size, 1), 8 * size, 2)
        up = pltpu.roll(pltpu.roll(tile, size, 1), 128 - 8 * size, 2)
        tile = jnp.where(row_bit == lane_bit, tile, jnp.where(row_bit == 0, down, up))
    return tile


def kernel(
    shards, groups, offsets, coulomb, pair_vc, dens_cc, dens_vv, screen,
    out, cc_land, vv_land,
    both, ex_send, ex_recv, wide, vv_here, cc_here, image, rows,
    send_sem, recv_sem, ka_send, ka_recv, own_sem, load_sem,
):
    me = lax.axis_index("ga")
    my_ka = lax.axis_index("ka")
    local_k, slab, _ = pair_vc.shape
    few_k = local_k // shards
    quarter = slab // groups
    steps = step_order(shards)
    lane = lax.broadcasted_iota(jnp.int32, (64, 128), 1)
    sign = jnp.where(lane < 64, 1.0, -1.0)

    barrier = pltpu.get_barrier_semaphore()
    for step in range(1, shards):
        pl.semaphore_signal(
            barrier, inc=1, device_id={"ga": (me + step) % shards}, device_id_type=MESH
        )
    for step in range(1, groups):
        pl.semaphore_signal(
            barrier, inc=1, device_id={"ka": (my_ka + step) % groups}, device_id_type=MESH
        )
    pl.semaphore_wait(barrier, shards - 1 + groups - 1)

    def own(index, source, target):
        return pltpu.make_async_copy(source, target, own_sem.at[index])

    def to_ga(kind, step, source, target):
        return pltpu.make_async_remote_copy(
            src_ref=source,
            dst_ref=target,
            send_sem=send_sem.at[kind, step],
            recv_sem=recv_sem.at[kind, step],
            device_id={"ga": (me + step) % shards},
            device_id_type=MESH,
        )

    def to_ka(index, step, source, target):
        return pltpu.make_async_remote_copy(
            src_ref=source,
            dst_ref=target,
            send_sem=ka_send.at[index],
            recv_sem=ka_recv.at[index],
            device_id={"ka": (my_ka + step) % groups},
            device_id_type=MESH,
        )

    def dens_copies(kind, dens, land, offset):
        return [
            to_ga(
                kind,
                step,
                dens.at[offset, pl.ds(((me + step) % shards) * few_k, few_k)],
                land.at[offset, :, me],
            )
            for step in steps
        ]

    ahead = to_ka(0, groups - 1, pair_vc, both.at[pl.ds(local_k, local_k)])
    ahead.start()
    my_rows = screen.at[:, pl.ds(my_ka * quarter, quarter)]
    screen_ga = [to_ga(4, step, my_rows, wide.at[:, me, my_ka]) for step in steps]
    for copy in screen_ga:
        copy.start()
    mine = [
        own(0, pair_vc, both.at[pl.ds(0, local_k)]),
        own(1, my_rows, wide.at[:, me, my_ka]),
    ]
    for offset in range(NOFF):
        for index, dens, land in ((2, dens_cc, cc_land), (3, dens_vv, vv_land)):
            mine.append(
                own(
                    index + 2 * offset,
                    dens.at[offset, pl.ds(me * few_k, few_k)],
                    land.at[offset, :, me],
                )
            )
    for copy in mine:
        copy.start()

    vv_copies = [dens_copies(offset, dens_vv, vv_land, offset) for offset in range(NOFF)]
    cc_copies = [dens_copies(2 + offset, dens_cc, cc_land, offset) for offset in range(NOFF)]
    queue = []
    for offset in range(NOFF):
        queue += vv_copies[offset] + cc_copies[offset]
    sent = [0, 0]

    def finish(count):
        for _ in range(count):
            queue[sent[1]].wait_send()
            sent[1] += 1
            if sent[0] < len(queue):
                queue[sent[0]].start()
                sent[0] += 1

    while sent[0] < min(WINDOW, len(queue)):
        queue[sent[0]].start()
        sent[0] += 1

    for copy in screen_ga:
        copy.wait_recv()
    mine[1].wait()
    screen_ka = [
        to_ka(step, step, wide.at[:, :, my_ka], wide.at[:, :, my_ka])
        for step in range(1, groups)
    ]
    for copy in screen_ka:
        copy.start()

    mine[0].wait()
    ahead.wait_recv()

    def one_exchange(k, carry):
        scaled = (coulomb[...] * both[k].astype(jnp.float32)).astype(jnp.bfloat16)
        row, column = k // NKY, k % NKY
        for offset in range(NOFF):
            moved_column = column + offsets[offset, 1]
            moved_column = jnp.where(moved_column >= NKY, moved_column - NKY, moved_column)
            partner = (row + offsets[offset, 0]) * NKY + moved_column
            full = over_rows(scaled, both[partner])
            summed = full[:64] + sign * pltpu.roll(full[64:], 64, 1)
            ex_send[offset, k] = summed.astype(jnp.bfloat16)
        return carry

    lax.fori_loop(0, local_k, one_exchange, 0)
    ex_copies = [
        to_ga(
            5,
            step,
            ex_send.at[:, pl.ds(((me + step) % shards) * few_k, few_k)],
            ex_recv.at[step],
        )
        for step in steps
    ]
    for copy in ex_copies:
        copy.start()

    together = 2 if few_k % 2 == 0 else 1
    big = slab * shards

    for offset in range(NOFF):
        finish(len(steps))
        for copy in vv_copies[offset]:
            copy.wait_recv()
        mine[3 + 2 * offset].wait()
        load = pltpu.make_async_copy(vv_land.at[offset], vv_here, load_sem.at[0])
        load.start()
        if offset == 0:
            for copy in screen_ka:
                copy.wait_recv()
        load.wait()

        def one_image(index, carry, offset=offset):
            first = (index // shards) * together
            part = index % shards
            right = jnp.concatenate(
                [vv_here[first + i].reshape(big, 128) for i in range(together)], axis=1
            )
            left = wide[offset, part].reshape(slab, big)
            made = jnp.dot(left, right, preferred_element_type=jnp.float32)
            made = made.astype(jnp.bfloat16)
            for i in range(together):
                image[first + i, part] = made[:, i * 128 : (i + 1) * 128]
            return carry

        lax.fori_loop(0, few_k // together * shards, one_image, 0)

        finish(len(steps))
        if offset == 0:
            for copy in ex_copies:
                copy.wait_recv()
        for copy in cc_copies[offset]:
            copy.wait_recv()
        mine[2 + 2 * offset].wait()
        load = pltpu.make_async_copy(cc_land.at[offset], cc_here, load_sem.at[1])
        load.start()
        load.wait()

        def one_direct(k, carry, offset=offset):
            full = over_rows(image[k].reshape(big, 128), cc_here[k].reshape(big, 128))
            summed = pltpu.roll(full[64:], 64, 1) + sign * full[:64]
            direct = block_transpose(summed.reshape(8, 8, 128)).reshape(64, 128)
            exchange = ex_send[offset, me * few_k + k].astype(jnp.float32)
            for step in range(1, shards):
                exchange = exchange + ex_recv[step, offset, k].astype(jnp.float32)
            rows[k] = 2.0 * exchange - direct
            return carry

        lax.fori_loop(0, few_k, one_direct, 0)
        narrow = lax.broadcasted_iota(jnp.int32, (few_k, 128), 1) < 64
        for pair in range(32):
            even, odd = rows[:, 2 * pair, :], rows[:, 2 * pair + 1, :]
            place = pl.ds(pair * 128, 128)
            out[offset, 0, :, place] = jnp.where(narrow, even, pltpu.roll(odd, 64, 1))
            out[offset, 1, :, place] = jnp.where(narrow, pltpu.roll(even, 64, 1), odd)

    ahead.wait_send()
    for copy in screen_ga + screen_ka + ex_copies:
        copy.wait_send()


def local(shards, groups, pair_vc, coulomb, dens_cc, dens_vv, screen, offsets):
    local_k, slab, width = pair_vc.shape
    few_k = local_k // shards
    big = slab * shards
    spread = jnp.broadcast_to(coulomb[:, None], (slab, width))
    land = jax.ShapeDtypeStruct((NOFF, few_k, shards, slab, width), jnp.bfloat16)
    anywhere = pl.BlockSpec(memory_space=pl.ANY)
    in_vmem = pl.BlockSpec(memory_space=pltpu.VMEM)
    flops = 2 * NOFF * (few_k * big * big * width + 2 * few_k * big * width * width)
    result = pl.pallas_call(
        functools.partial(kernel, shards, groups),
        out_shape=[
            jax.ShapeDtypeStruct((NOFF, 2, few_k, 4096), jnp.float32),
            land,
            land,
        ],
        in_specs=[pl.BlockSpec(memory_space=pltpu.SMEM), in_vmem] + [anywhere] * 4,
        out_specs=[in_vmem, anywhere, anywhere],
        scratch_shapes=[
            pltpu.VMEM((2 * local_k, slab, width), jnp.bfloat16),
            pltpu.VMEM((NOFF, local_k, 64, 128), jnp.bfloat16),
            pltpu.VMEM((shards, NOFF, few_k, 64, 128), jnp.bfloat16),
            pltpu.VMEM((NOFF, shards, groups, slab // groups, big), jnp.bfloat16),
            pltpu.VMEM((few_k, shards, slab, width), jnp.bfloat16),
            pltpu.VMEM((few_k, shards, slab, width), jnp.bfloat16),
            pltpu.VMEM((few_k, shards, slab, width), jnp.bfloat16),
            pltpu.VMEM((few_k, 64, 128), jnp.float32),
            pltpu.SemaphoreType.DMA((6, shards)),
            pltpu.SemaphoreType.DMA((6, shards)),
            pltpu.SemaphoreType.DMA((groups,)),
            pltpu.SemaphoreType.DMA((groups,)),
            pltpu.SemaphoreType.DMA((6,)),
            pltpu.SemaphoreType.DMA((2,)),
        ],
        compiler_params=pltpu.CompilerParams(
            collective_id=0, has_side_effects=True, vmem_limit_bytes=60 * 1024 * 1024
        ),
        cost_estimate=pl.CostEstimate(flops=flops, bytes_accessed=80_000_000, transcendentals=0),
        name="bse_blocks",
    )(offsets, spread, pair_vc, dens_cc, dens_vv, screen)
    return result[0]


def solution(mesh):
    placed = (
        P("ka", "ga", None),
        P("ga"),
        P(None, "ka", "ga", None),
        P(None, "ka", "ga", None),
        P(None, "ga", None),
        P(),
    )
    return jax.shard_map(
        functools.partial(local, mesh.shape["ga"], mesh.shape["ka"]),
        mesh=mesh,
        in_specs=placed,
        out_specs=P(None, None, ("ka", "ga"), None),
        check_vma=False,
    )
```

time: 1250 us -> 720 us (0.58); the launches traced: 1240 us -> 719 us
  waiting for transfers between devices: 963 us -> 0 us
  Pallas kernels: 0 us -> 715 us
  local copies, waits for them, and re-layouts: 118 us -> 4.14 us
  other arithmetic: 68 us -> 0 us
  matrix products: 51.5 us -> 0 us
  between operations: 21.3 us -> 0.01 us
  starting transfers between devices: 14 us -> 0 us
    pallas_call x0 -> x1, Pallas kernels: none -> 715 us  [local(): pl.pallas_call(functools.partial(kernel, shards, groups), out_shape=[jax....]
    unnamed x4 -> x0, waiting for transfers between devices: 474 us -> none
    all_to_all x2 -> x0, waiting for transfers between devices: 244 us -> none  [the longest x1 244 us: local(): lax.all_to_all(dens_cc, 'ga', split_axis=1, concat_axis=2, tiled=True)]
    all_gather x2 -> x0, waiting for transfers between devices: 183 us -> none  [local(): lax.all_gather(screen[offset_index], 'ga', axis=0, tiled=True)]
    ppermute x1 -> x0, waiting for transfers between devices: 62.6 us -> none  [from_behind(): lax.ppermute(array, axis, [(i, (i + by) % length) for i in range(length)])]
    dot_general x4 -> x0, matrix products: 51.5 us -> none  [pair_products(): jnp.einsum('kgp,kgq->kpq', left_side, right_side, preferred_element_type=...]
    another operation x5 -> x0, other arithmetic: 27.5 us -> none  [the longest x3 20.9 us: summed_exchange(): jnp.stack([pair_products(scaled, moved[offset_index]) for offset_index in...]
    unnamed x25 -> x0, local copies, waits for them, and re-layouts: 25.2 us -> none
  transfers between devices with their start and end apart: 6 -> 0, of which waited for: 5 -> 0; matrix products, arithmetic and copies ran while one was open for 13% -> 0% of each run, Pallas kernels for 0% -> 0%
where the time goes in v1:
time: 720 us; the launch traced here: 719 us
  Pallas kernels  715 us (99%)
    pallas_call x1, Pallas kernels, local(): pl.pallas_call(functools.partial(kernel, shards, groups), out_shape=[jax....  715 us

profile of v1, /device:TPU:13, one launch (start us, length us, event | category | flops | bytes accessed | tf_op | source)
XLA Modules:
  0.0 719.4 jit_solution(15118387409194943880)
XLA Ops:
  0.0 1.4 broadcast_in_dim.2.coulomb
  1.4 715.3 %bse_blocks.1 = (f32[2,2,12,4096]{3,2,1,0:T(8,128)}, bf16[2,12,8,256,128]{4,3,2,1,0:T(8,128)(2,1)}, bf16[2,12,8,256,128]{4,3,2,1,0:T(8,128)(2,1)}) custom-call(s32[2,2]{1,0:T(2,128)} %offsets.1, f32[256,128]{1,0:T(8,128)} %broadcast_in_dim.2.coulomb, bf16[96,256,128]{2,1,0:T(8,128)(2,1)} %pair_vc.1, bf16[2,96,256,128]{3,2,1,0:T(8,128)(2,1)} %dens_cc.1, ...), custom_call_target="tpu_custom_call" | custom-call | flops 28991029248 | bytes 80000000 | tf_op jit(solution)/shard_map/bse_blocks/pallas_call | solution.py:258
  716.7 2.7 copy.7

commit v2 on v1

--- a/solution.py
+++ b/solution.py
@@ -46,7 +46,7 @@
 def kernel(
     shards, groups, offsets, coulomb, pair_vc, dens_cc, dens_vv, screen,
     out, cc_land, vv_land,
-    both, ex_send, ex_recv, wide, vv_here, cc_here, image, rows,
+    both, ex, ex_recv, far_send, far_recv, wide, vv_here, cc_here, image, rows,
     send_sem, recv_sem, ka_send, ka_recv, own_sem, load_sem,
 ):
     me = lax.axis_index("ga")
@@ -82,6 +82,19 @@
             device_id_type=MESH,
         )
 
+    def partner_of(distance):
+        return me + distance - 2 * distance * ((me // distance) % 2)
+
+    def to_partner(kind, index, distance, source, target):
+        return pltpu.make_async_remote_copy(
+            src_ref=source,
+            dst_ref=target,
+            send_sem=send_sem.at[kind, index],
+            recv_sem=recv_sem.at[kind, index],
+            device_id={"ga": partner_of(distance)},
+            device_id_type=MESH,
+        )
+
     def to_ka(index, step, source, target):
         return pltpu.make_async_remote_copy(
             src_ref=source,
@@ -106,8 +119,20 @@
     ahead = to_ka(0, groups - 1, pair_vc, both.at[pl.ds(local_k, local_k)])
     ahead.start()
     my_rows = screen.at[:, pl.ds(my_ka * quarter, quarter)]
-    screen_ga = [to_ga(4, step, my_rows, wide.at[:, me, my_ka]) for step in steps]
-    for copy in screen_ga:
+    screen_hops = []
+    distance = shards // 2
+    taken = 0
+    while distance >= 1:
+        hop = []
+        for i in range(shards // (2 * distance)):
+            block = me % (2 * distance) + 2 * distance * i
+            place = wide.at[:, block, my_ka]
+            hop.append(to_partner(4, taken, distance, my_rows if taken == 0 else place, place))
+            taken += 1
+        screen_hops.append(hop)
+        distance //= 2
+    screen_ga = sum(screen_hops, [])
+    for copy in screen_hops[0]:
         copy.start()
     mine = [
         own(0, pair_vc, both.at[pl.ds(0, local_k)]),
@@ -144,9 +169,13 @@
         queue[sent[0]].start()
         sent[0] += 1
 
-    for copy in screen_ga:
-        copy.wait_recv()
     mine[1].wait()
+    for index, hop in enumerate(screen_hops):
+        for copy in hop:
+            copy.wait_recv()
+        if index + 1 < len(screen_hops):
+            for copy in screen_hops[index + 1]:
+                copy.start()
     screen_ka = [
         to_ka(step, step, wide.at[:, :, my_ka], wide.at[:, :, my_ka])
         for step in range(1, groups)
@@ -166,21 +195,57 @@
             partner = (row + offsets[offset, 0]) * NKY + moved_column
             full = over_rows(scaled, both[partner])
             summed = full[:64] + sign * pltpu.roll(full[64:], 64, 1)
-            ex_send[offset, k] = summed.astype(jnp.bfloat16)
+            ex[offset, k // few_k, k % few_k] = summed
         return carry
 
     lax.fori_loop(0, local_k, one_exchange, 0)
-    ex_copies = [
-        to_ga(
-            5,
-            step,
-            ex_send.at[:, pl.ds(((me + step) % shards) * few_k, few_k)],
-            ex_recv.at[step],
-        )
-        for step in steps
-    ]
-    for copy in ex_copies:
-        copy.start()
+    hops = []
+    distance = 1
+    taken = 0
+    while distance < shards:
+        hop = []
+        for i in range(shards // (2 * distance)):
+            block = partner_of(distance) % (2 * distance) + 2 * distance * i
+            if 2 * distance < shards:
+                source, target = ex.at[:, block], ex_recv.at[taken]
+            else:
+                source, target = far_send, far_recv
+            hop.append((to_partner(5, taken, distance, source, target), taken, distance, i))
+            taken += 1
+        hops.append(hop)
+        distance *= 2
+    ex_copies = [copy for hop in hops for copy, _, _, _ in hop]
+
+    def start_hop(index):
+        if index + 1 == len(hops):
+            far_send[...] = ex[:, partner_of(shards // 2)].astype(jnp.bfloat16)
+        for copy, _, _, _ in hops[index]:
+            copy.start()
+
+    def end_hop(index):
+        for copy, slot, distance, i in hops[index]:
+            copy.wait()
+            if index + 1 < len(hops):
+                block = me % (2 * distance) + 2 * distance * i
+
+                def add(k, carry, slot=slot, block=block):
+                    for offset in range(NOFF):
+                        ex[offset, block, k] = ex[offset, block, k] + ex_recv[slot, offset, k]
+                    return carry
+
+                lax.fori_loop(0, few_k, add, 0)
+
+    start_hop(0)
+
+    rows[...] = jnp.zeros_like(rows)
+
+    def write_out(offset):
+        narrow = lax.broadcasted_iota(jnp.int32, (few_k, 128), 1) < 64
+        for pair in range(32):
+            even, odd = rows[offset, :, 2 * pair, :], rows[offset, :, 2 * pair + 1, :]
+            place = pl.ds(pair * 128, 128)
+            out[offset, 0, :, place] = jnp.where(narrow, even, pltpu.roll(odd, 64, 1))
+            out[offset, 1, :, place] = jnp.where(narrow, pltpu.roll(even, 64, 1), odd)
 
     together = 2 if few_k % 2 == 0 else 1
     big = slab * shards
@@ -211,11 +276,22 @@
             return carry
 
         lax.fori_loop(0, few_k // together * shards, one_image, 0)
+        if offset == 0:
+            end_hop(0)
+            start_hop(1)
+        else:
+            end_hop(len(hops) - 1)
+
+            def add_far(k, carry):
+                for each in range(NOFF):
+                    total = ex[each, me, k] + far_recv[each, k].astype(jnp.float32)
+                    rows[each, k] = rows[each, k] + 2.0 * total
+                return carry
+
+            lax.fori_loop(0, few_k, add_far, 0)
+            write_out(0)
 
         finish(len(steps))
-        if offset == 0:
-            for copy in ex_copies:
-                copy.wait_recv()
         for copy in cc_copies[offset]:
             copy.wait_recv()
         mine[2 + 2 * offset].wait()
@@ -227,22 +303,18 @@
             full = over_rows(image[k].reshape(big, 128), cc_here[k].reshape(big, 128))
             summed = pltpu.roll(full[64:], 64, 1) + sign * full[:64]
             direct = block_transpose(summed.reshape(8, 8, 128)).reshape(64, 128)
-            exchange = ex_send[offset, me * few_k + k].astype(jnp.float32)
-            for step in range(1, shards):
-                exchange = exchange + ex_recv[step, offset, k].astype(jnp.float32)
-            rows[k] = 2.0 * exchange - direct
+            rows[offset, k] = rows[offset, k] - direct
             return carry
 
         lax.fori_loop(0, few_k, one_direct, 0)
-        narrow = lax.broadcasted_iota(jnp.int32, (few_k, 128), 1) < 64
-        for pair in range(32):
-            even, odd = rows[:, 2 * pair, :], rows[:, 2 * pair + 1, :]
-            place = pl.ds(pair * 128, 128)
-            out[offset, 0, :, place] = jnp.where(narrow, even, pltpu.roll(odd, 64, 1))
-            out[offset, 1, :, place] = jnp.where(narrow, pltpu.roll(even, 64, 1), odd)
+        if offset == 0:
+            for index in range(1, len(hops) - 1):
+                end_hop(index)
+                start_hop(index + 1)
+    write_out(1)
 
     ahead.wait_send()
-    for copy in screen_ga + screen_ka + ex_copies:
+    for copy in screen_ga + screen_ka:
         copy.wait_send()
 
 
@@ -266,13 +338,15 @@
         out_specs=[in_vmem, anywhere, anywhere],
         scratch_shapes=[
             pltpu.VMEM((2 * local_k, slab, width), jnp.bfloat16),
-            pltpu.VMEM((NOFF, local_k, 64, 128), jnp.bfloat16),
-            pltpu.VMEM((shards, NOFF, few_k, 64, 128), jnp.bfloat16),
+            pltpu.VMEM((NOFF, shards, few_k, 64, 128), jnp.float32),
+            pltpu.VMEM((shards - 2, NOFF, few_k, 64, 128), jnp.float32),
+            pltpu.VMEM((NOFF, few_k, 64, 128), jnp.bfloat16),
+            pltpu.VMEM((NOFF, few_k, 64, 128), jnp.bfloat16),
             pltpu.VMEM((NOFF, shards, groups, slab // groups, big), jnp.bfloat16),
             pltpu.VMEM((few_k, shards, slab, width), jnp.bfloat16),
             pltpu.VMEM((few_k, shards, slab, width), jnp.bfloat16),
             pltpu.VMEM((few_k, shards, slab, width), jnp.bfloat16),
-            pltpu.VMEM((few_k, 64, 128), jnp.float32),
+            pltpu.VMEM((NOFF, few_k, 64, 128), jnp.float32),
             pltpu.SemaphoreType.DMA((6, shards)),
             pltpu.SemaphoreType.DMA((6, shards)),
             pltpu.SemaphoreType.DMA((groups,)),
@@ -281,7 +355,7 @@
             pltpu.SemaphoreType.DMA((2,)),
         ],
         compiler_params=pltpu.CompilerParams(
-            collective_id=0, has_side_effects=True, vmem_limit_bytes=60 * 1024 * 1024
+            collective_id=0, has_side_effects=True, vmem_limit_bytes=62 * 1024 * 1024
         ),
         cost_estimate=pl.CostEstimate(flops=flops, bytes_accessed=80_000_000, transcendentals=0),
         name="bse_blocks",

time: 720 us -> 624 us (0.87)
  Pallas kernels: 715 us -> 620 us
    pallas_call x1, Pallas kernels: 715 us -> 620 us  [local(): pl.pallas_call(functools.partial(kernel, shards, groups), out_shape=[jax....]
where the time goes in v2:
time: 624 us
  Pallas kernels  620 us (99%)
    pallas_call x1, Pallas kernels, local(): pl.pallas_call(functools.partial(kernel, shards, groups), out_shape=[jax....  620 us

profile of v2, /device:TPU:13, one launch (start us, length us, event | category | flops | bytes accessed | tf_op | source)
XLA Modules:
  0.0 624.0 jit_solution(17438306421670059387)
XLA Ops:
  0.0 1.4 broadcast_in_dim.2.coulomb
  1.4 619.9 %bse_blocks.1 = (f32[2,2,12,4096]{3,2,1,0:T(8,128)}, bf16[2,12,8,256,128]{4,3,2,1,0:T(8,128)(2,1)}, bf16[2,12,8,256,128]{4,3,2,1,0:T(8,128)(2,1)}) custom-call(s32[2,2]{1,0:T(2,128)} %offsets.1, f32[256,128]{1,0:T(8,128)} %broadcast_in_dim.2.coulomb, bf16[96,256,128]{2,1,0:T(8,128)(2,1)} %pair_vc.1, bf16[2,96,256,128]{3,2,1,0:T(8,128)(2,1)} %dens_cc.1, ...), custom_call_target="tpu_custom_call" | custom-call | flops 28991029248 | bytes 80000000 | tf_op jit(solution)/shard_map/bse_blocks/pallas_call | solution.py:330
  621.3 2.7 copy.7

commit v3 on v2

--- a/solution.py
+++ b/solution.py
@@ -11,7 +11,6 @@
 NC = 8
 NKY = 24
 NOFF = 2
-WINDOW = 10
 MESH = pl.DeviceIdType.MESH
 
 
@@ -46,7 +45,7 @@
 def kernel(
     shards, groups, offsets, coulomb, pair_vc, dens_cc, dens_vv, screen,
     out, cc_land, vv_land,
-    both, ex, ex_recv, far_send, far_recv, wide, vv_here, cc_here, image, rows,
+    both, ex, ex_recv, far_send, far_recv, wide, vv_here, cc_here, image, totals, rows,
     send_sem, recv_sem, ka_send, ka_recv, own_sem, load_sem,
 ):
     me = lax.axis_index("ga")
@@ -165,7 +164,7 @@
                 queue[sent[0]].start()
                 sent[0] += 1
 
-    while sent[0] < min(WINDOW, len(queue)):
+    while sent[0] < 2 * len(steps):
         queue[sent[0]].start()
         sent[0] += 1
 
@@ -291,16 +290,36 @@
             lax.fori_loop(0, few_k, add_far, 0)
             write_out(0)
 
-        finish(len(steps))
-        for copy in cc_copies[offset]:
-            copy.wait_recv()
+        def bring(source, offset=offset):
+            return pltpu.make_async_copy(
+                cc_land.at[offset, :, source], cc_here.at[:, source], load_sem.at[1]
+            )
+
+        def add_slab(source):
+            def one_slab(k, carry):
+                totals[k] = totals[k] + over_rows(image[k, source], cc_here[k, source])
+                return carry
+
+            lax.fori_loop(0, few_k, one_slab, 0)
+
+        totals[...] = jnp.zeros_like(totals)
         mine[2 + 2 * offset].wait()
-        load = pltpu.make_async_copy(cc_land.at[offset], cc_here, load_sem.at[1])
+        load = bring(me)
         load.start()
         load.wait()
+        add_slab(me)
+        for step, copy in zip(steps, cc_copies[offset]):
+            copy.wait_recv()
+            source = (me + shards - step) % shards
+            load = bring(source)
+            load.start()
+            load.wait()
+            add_slab(source)
+            if offset == 0:
+                finish(1)
 
         def one_direct(k, carry, offset=offset):
-            full = over_rows(image[k].reshape(big, 128), cc_here[k].reshape(big, 128))
+            full = totals[k]
             summed = pltpu.roll(full[64:], 64, 1) + sign * full[:64]
             direct = block_transpose(summed.reshape(8, 8, 128)).reshape(64, 128)
             rows[offset, k] = rows[offset, k] - direct
@@ -313,6 +332,7 @@
                 start_hop(index + 1)
     write_out(1)
 
+    finish(len(steps))
     ahead.wait_send()
     for copy in screen_ga + screen_ka:
         copy.wait_send()
@@ -346,6 +366,7 @@
             pltpu.VMEM((few_k, shards, slab, width), jnp.bfloat16),
             pltpu.VMEM((few_k, shards, slab, width), jnp.bfloat16),
             pltpu.VMEM((few_k, shards, slab, width), jnp.bfloat16),
+            pltpu.VMEM((few_k, 128, 128), jnp.float32),
             pltpu.VMEM((NOFF, few_k, 64, 128), jnp.float32),
             pltpu.SemaphoreType.DMA((6, shards)),
             pltpu.SemaphoreType.DMA((6, shards)),

time: 624 us -> 666 us (1.067)
  Pallas kernels: 620 us -> 659 us
    pallas_call x1, Pallas kernels: 620 us -> 659 us  [local(): pl.pallas_call(functools.partial(kernel, shards, groups), out_shape=[jax....]
where the time goes in v3:
time: 666 us; the launch traced here: 663 us
  Pallas kernels  659 us (99%)
    pallas_call x1, Pallas kernels, local(): pl.pallas_call(functools.partial(kernel, shards, groups), out_shape=[jax....  659 us

profile of v3, /device:TPU:13, one launch (start us, length us, event | category | flops | bytes accessed | tf_op | source)
XLA Modules:
  0.0 662.8 jit_solution(3406780860204016193)
XLA Ops:
  0.0 1.4 broadcast_in_dim.2.coulomb
  1.4 658.7 %bse_blocks.1 = (f32[2,2,12,4096]{3,2,1,0:T(8,128)}, bf16[2,12,8,256,128]{4,3,2,1,0:T(8,128)(2,1)}, bf16[2,12,8,256,128]{4,3,2,1,0:T(8,128)(2,1)}) custom-call(s32[2,2]{1,0:T(2,128)} %offsets.1, f32[256,128]{1,0:T(8,128)} %broadcast_in_dim.2.coulomb, bf16[96,256,128]{2,1,0:T(8,128)(2,1)} %pair_vc.1, bf16[2,96,256,128]{3,2,1,0:T(8,128)(2,1)} %dens_cc.1, ...), custom_call_target="tpu_custom_call" | custom-call | flops 28991029248 | bytes 80000000 | tf_op jit(solution)/shard_map/bse_blocks/pallas_call | solution.py:350
  660.1 2.7 copy.7

commit v4 on v3

--- a/solution.py
+++ b/solution.py
@@ -11,15 +11,15 @@
 NC = 8
 NKY = 24
 NOFF = 2
+WINDOW = 6
 MESH = pl.DeviceIdType.MESH
 
 
 def step_order(length):
-    order = []
-    for i in range(length):
-        step = length // 2 + (i + 1) // 2 * (1 if i % 2 else -1)
-        if 0 < step < length:
-            order.append(step)
+    half = length // 2
+    order = [half]
+    for near in range(1, half):
+        order += [near, half + near]
     return order
 
 
@@ -71,18 +71,16 @@
     def own(index, source, target):
         return pltpu.make_async_copy(source, target, own_sem.at[index])
 
-    def to_ga(kind, step, source, target):
-        return pltpu.make_async_remote_copy(
-            src_ref=source,
-            dst_ref=target,
-            send_sem=send_sem.at[kind, step],
-            recv_sem=recv_sem.at[kind, step],
-            device_id={"ga": (me + step) % shards},
-            device_id_type=MESH,
-        )
+    def flipped(index, distance, length):
+        bit = 1
+        while bit < length:
+            if distance & bit:
+                index = index + bit - 2 * bit * ((index // bit) % 2)
+            bit *= 2
+        return index
 
     def partner_of(distance):
-        return me + distance - 2 * distance * ((me // distance) % 2)
+        return flipped(me, distance, shards)
 
     def to_partner(kind, index, distance, source, target):
         return pltpu.make_async_remote_copy(
@@ -94,28 +92,29 @@
             device_id_type=MESH,
         )
 
-    def to_ka(index, step, source, target):
+    def to_ka(index, peer, source, target):
         return pltpu.make_async_remote_copy(
             src_ref=source,
             dst_ref=target,
             send_sem=ka_send.at[index],
             recv_sem=ka_recv.at[index],
-            device_id={"ka": (my_ka + step) % groups},
+            device_id={"ka": peer},
             device_id_type=MESH,
         )
 
     def dens_copies(kind, dens, land, offset):
         return [
-            to_ga(
+            to_partner(
                 kind,
                 step,
-                dens.at[offset, pl.ds(((me + step) % shards) * few_k, few_k)],
+                step,
+                dens.at[offset, pl.ds(partner_of(step) * few_k, few_k)],
                 land.at[offset, :, me],
             )
             for step in steps
         ]
 
-    ahead = to_ka(0, groups - 1, pair_vc, both.at[pl.ds(local_k, local_k)])
+    ahead = to_ka(0, (my_ka + groups - 1) % groups, pair_vc, both.at[pl.ds(local_k, local_k)])
     ahead.start()
     my_rows = screen.at[:, pl.ds(my_ka * quarter, quarter)]
     screen_hops = []
@@ -164,7 +163,7 @@
                 queue[sent[0]].start()
                 sent[0] += 1
 
-    while sent[0] < 2 * len(steps):
+    while sent[0] < min(WINDOW, len(queue)):
         queue[sent[0]].start()
         sent[0] += 1
 
@@ -175,12 +174,21 @@
         if index + 1 < len(screen_hops):
             for copy in screen_hops[index + 1]:
                 copy.start()
-    screen_ka = [
-        to_ka(step, step, wide.at[:, :, my_ka], wide.at[:, :, my_ka])
-        for step in range(1, groups)
-    ]
-    for copy in screen_ka:
+    screen_ka_hops = []
+    distance = groups // 2
+    taken = 1
+    while distance >= 1:
+        hop = []
+        for i in range(groups // (2 * distance)):
+            part = wide.at[:, :, my_ka % (2 * distance) + 2 * distance * i]
+            hop.append(to_ka(taken, flipped(my_ka, distance, groups), part, part))
+            taken += 1
+        screen_ka_hops.append(hop)
+        distance //= 2
+    screen_ka = sum(screen_ka_hops, [])
+    for copy in screen_ka_hops[0]:
         copy.start()
+    finish(2)
 
     mine[0].wait()
     ahead.wait_recv()
@@ -197,7 +205,14 @@
             ex[offset, k // few_k, k % few_k] = summed
         return carry
 
-    lax.fori_loop(0, local_k, one_exchange, 0)
+    lax.fori_loop(0, local_k // 2, one_exchange, 0)
+    finish(1)
+    lax.fori_loop(local_k // 2, local_k, one_exchange, 0)
+    for index in range(1, len(screen_ka_hops)):
+        for copy in screen_ka_hops[index - 1]:
+            copy.wait_recv()
+        for copy in screen_ka_hops[index]:
+            copy.start()
     hops = []
     distance = 1
     taken = 0
@@ -250,14 +265,14 @@
     big = slab * shards
 
     for offset in range(NOFF):
-        finish(len(steps))
+        finish(len(steps) - 3 if offset == 0 else len(steps))
         for copy in vv_copies[offset]:
             copy.wait_recv()
         mine[3 + 2 * offset].wait()
         load = pltpu.make_async_copy(vv_land.at[offset], vv_here, load_sem.at[0])
         load.start()
         if offset == 0:
-            for copy in screen_ka:
+            for copy in screen_ka_hops[-1]:
                 copy.wait_recv()
         load.wait()
 
@@ -309,14 +324,13 @@
         load.wait()
         add_slab(me)
         for step, copy in zip(steps, cc_copies[offset]):
+            finish(1)
             copy.wait_recv()
-            source = (me + shards - step) % shards
+            source = partner_of(step)
             load = bring(source)
             load.start()
             load.wait()
             add_slab(source)
-            if offset == 0:
-                finish(1)
 
         def one_direct(k, carry, offset=offset):
             full = totals[k]
@@ -332,7 +346,6 @@
                 start_hop(index + 1)
     write_out(1)
 
-    finish(len(steps))
     ahead.wait_send()
     for copy in screen_ga + screen_ka:
         copy.wait_send()

time: 666 us -> 714 us (1.072)
  Pallas kernels: 659 us -> 702 us
    pallas_call x1, Pallas kernels: 659 us -> 702 us  [local(): pl.pallas_call(functools.partial(kernel, shards, groups), out_shape=[jax....]
where the time goes in v4:
time: 714 us; the launch traced here: 707 us
  Pallas kernels  702 us (98%)
    pallas_call x1, Pallas kernels, local(): pl.pallas_call(functools.partial(kernel, shards, groups), out_shape=[jax....  702 us

profile of v4, /device:TPU:13, one launch (start us, length us, event | category | flops | bytes accessed | tf_op | source)
XLA Modules:
  0.0 706.5 jit_solution(10459659078654680074)
XLA Ops:
  0.0 1.4 broadcast_in_dim.2.coulomb
  1.4 702.4 %bse_blocks.1 = (f32[2,2,12,4096]{3,2,1,0:T(8,128)}, bf16[2,12,8,256,128]{4,3,2,1,0:T(8,128)(2,1)}, bf16[2,12,8,256,128]{4,3,2,1,0:T(8,128)(2,1)}) custom-call(s32[2,2]{1,0:T(2,128)} %offsets.1, f32[256,128]{1,0:T(8,128)} %broadcast_in_dim.2.coulomb, bf16[96,256,128]{2,1,0:T(8,128)(2,1)} %pair_vc.1, bf16[2,96,256,128]{3,2,1,0:T(8,128)(2,1)} %dens_cc.1, ...), custom_call_target="tpu_custom_call" | custom-call | flops 28991029248 | bytes 80000000 | tf_op jit(solution)/shard_map/bse_blocks/pallas_call | solution.py:363
  703.8 2.7 copy.7

commit v5 on v2

--- a/solution.py
+++ b/solution.py
@@ -95,13 +95,13 @@
             device_id_type=MESH,
         )
 
-    def to_ka(index, step, source, target):
+    def to_ka(index, peer, source, target):
         return pltpu.make_async_remote_copy(
             src_ref=source,
             dst_ref=target,
             send_sem=ka_send.at[index],
             recv_sem=ka_recv.at[index],
-            device_id={"ka": (my_ka + step) % groups},
+            device_id={"ka": peer},
             device_id_type=MESH,
         )
 
@@ -116,7 +116,7 @@
             for step in steps
         ]
 
-    ahead = to_ka(0, groups - 1, pair_vc, both.at[pl.ds(local_k, local_k)])
+    ahead = to_ka(0, (my_ka + groups - 1) % groups, pair_vc, both.at[pl.ds(local_k, local_k)])
     ahead.start()
     my_rows = screen.at[:, pl.ds(my_ka * quarter, quarter)]
     screen_hops = []
@@ -176,11 +176,20 @@
         if index + 1 < len(screen_hops):
             for copy in screen_hops[index + 1]:
                 copy.start()
-    screen_ka = [
-        to_ka(step, step, wide.at[:, :, my_ka], wide.at[:, :, my_ka])
-        for step in range(1, groups)
-    ]
-    for copy in screen_ka:
+    screen_ka_hops = []
+    distance = groups // 2
+    taken = 1
+    while distance >= 1:
+        hop = []
+        for i in range(groups // (2 * distance)):
+            part = wide.at[:, :, my_ka % (2 * distance) + 2 * distance * i]
+            peer = my_ka + distance - 2 * distance * ((my_ka // distance) % 2)
+            hop.append(to_ka(taken, peer, part, part))
+            taken += 1
+        screen_ka_hops.append(hop)
+        distance //= 2
+    screen_ka = sum(screen_ka_hops, [])
+    for copy in screen_ka_hops[0]:
         copy.start()
 
     mine[0].wait()
@@ -199,6 +208,11 @@
         return carry
 
     lax.fori_loop(0, local_k, one_exchange, 0)
+    for index in range(1, len(screen_ka_hops)):
+        for copy in screen_ka_hops[index - 1]:
+            copy.wait_recv()
+        for copy in screen_ka_hops[index]:
+            copy.start()
     hops = []
     distance = 1
     taken = 0
@@ -258,7 +272,7 @@
         load = pltpu.make_async_copy(vv_land.at[offset], vv_here, load_sem.at[0])
         load.start()
         if offset == 0:
-            for copy in screen_ka:
+            for copy in screen_ka_hops[-1]:
                 copy.wait_recv()
         load.wait()
 

time: 624 us -> 683 us (1.095)
  Pallas kernels: 620 us -> 677 us
    pallas_call x1, Pallas kernels: 620 us -> 677 us  [local(): pl.pallas_call(functools.partial(kernel, shards, groups), out_shape=[jax....]
where the time goes in v5:
time: 683 us; the launch traced here: 681 us
  Pallas kernels  677 us (99%)
    pallas_call x1, Pallas kernels, local(): pl.pallas_call(functools.partial(kernel, shards, groups), out_shape=[jax....  677 us

profile of v5, /device:TPU:13, one launch (start us, length us, event | category | flops | bytes accessed | tf_op | source)
XLA Modules:
  0.0 681.1 jit_solution(11159588851979720264)
XLA Ops:
  0.0 1.4 broadcast_in_dim.2.coulomb
  1.4 676.9 %bse_blocks.1 = (f32[2,2,12,4096]{3,2,1,0:T(8,128)}, bf16[2,12,8,256,128]{4,3,2,1,0:T(8,128)(2,1)}, bf16[2,12,8,256,128]{4,3,2,1,0:T(8,128)(2,1)}) custom-call(s32[2,2]{1,0:T(2,128)} %offsets.1, f32[256,128]{1,0:T(8,128)} %broadcast_in_dim.2.coulomb, bf16[96,256,128]{2,1,0:T(8,128)(2,1)} %pair_vc.1, bf16[2,96,256,128]{3,2,1,0:T(8,128)(2,1)} %dens_cc.1, ...), custom_call_target="tpu_custom_call" | custom-call | flops 28991029248 | bytes 80000000 | tf_op jit(solution)/shard_map/bse_blocks/pallas_call | solution.py:344
  678.4 2.7 copy.7
